TPU v7x, 256 devices: a whole 4x4x8 slice. The times are simulated.
256 devices in a mesh: img: 4 (over y_lo, core), cls: 64 (over x, z, y_hi).
Axes of the slice: x: 4, y: 4 (y_hi: 2, y_lo: 2; y = y_hi * 2 + y_lo), z: 8, core: 2. Of those that a mesh axis runs over, the one named last changes fastest.
Arguments:
- images: bfloat16 [16384, 4096], P(('img', 'cls')), may hold values from -64 to 64
- noise_var: float32 [16384], P(('img', 'cls')), may hold values from 16 to 128
- references: bfloat16 [256, 4096], P('cls'), may hold values from -3.5 to 3.5
- assign: int32 [16384, 4], P(('img', 'cls')), may hold values from 0 to 255, all different within a row; in each aligned block of 64 rows (0 to 63, 64 to 127, ...) at most 6 rows name the same one
- rotations: int32 [16384, 4], P(('img', 'cls')), may hold values from 0 to 7
Outputs:
- new_references: float32 [256, 4096], P('cls')
- log_evidence: float32 [16384], P(('img', 'cls'))
Inputs may be any that keep to these rules, and one draw needn't show every extreme that they name: `assign`: the candidates of one image are different classes. Within the rows of one device (aligned blocks of 64 rows) no class is named by more than 6 entries, and every class is named somewhere.
All inputs are finite; a program needn't handle non-finite values.
Results may differ from a plain program's by a relative error of at most 0.00085.
Values may be sent and summed in bfloat16 or wider, within the bound.
A program may use at most 128 MiB of HBM per device.

v0:
```python
import functools

import numpy as np
import jax
import jax.numpy as jnp
from jax import lax
from jax.experimental import pallas as pl
from jax.experimental.pallas import tpu as pltpu
from jax.sharding import PartitionSpec as P

SIDE = 64
K = 256
MESH = pl.DeviceIdType.MESH
F32 = jnp.float32
BF16 = jnp.bfloat16
prior_weight = 16.0

STRIP = ((0, 3), (1, 2))
FLIP_ROWS, FLIP_COLUMNS = 188, 67


def backward_turn(picture, turn):
    quarter = turn % 4
    result = np.rot90(picture, -quarter, axes=(-2, -1))
    return np.swapaxes(result, -1, -2) if turn >= 4 else result


def forms():
    number = np.arange(SIDE * SIDE).reshape(SIDE, SIDE)
    found = []
    for r in range(8):
        source = backward_turn(number, r)
        for swap in (0, 1):
            for rows in (0, 1):
                for columns in (0, 1):
                    trial = number.T if swap else number
                    trial = trial[::-1] if rows else trial
                    trial = trial[:, ::-1] if columns else trial
                    if (trial == source).all():
                        found.append((swap, rows * FLIP_ROWS ^ columns * FLIP_COLUMNS))
    assert len(found) == 8
    return found


FORMS = forms()


def wrap(value, size):
    return lax.rem(value + 2 * size, size)


def kernel(X, Z, images_hbm, refs_ref, noise_ref, assign_ref, turn_ref, out_ref, evidence_ref,
           im, inner, regroup, blocks, xall, xquad, turned, turned_quad, meta, ref_slab, zgot, zline, refs, own_scores,
           other_scores, per_class, tie, table, part, got_a, got_b, got_a2, got_b2, wts, tot, tot_y, tot_x, lines, zsend,
           zrecv, leave, slots, local_sem, send_sem, recv_sem):
    img, cls = lax.axis_index("img"), lax.axis_index("cls")
    yl, h = img // 2, lax.rem(img, 2)
    yh, z, x = lax.rem(cls, 2), lax.rem(cls // 2, Z), cls // (2 * Z)
    y = yh * 2 + yl
    xp, xb = x // 2, lax.rem(x, 2)
    xm, ym, xr, yr = x + 1 - 2 * xb, y + 1 - 2 * yl, 3 - x, 3 - y
    own_c = lax.rem((x + 1) // 2, 2) * 2 + lax.rem((y + 1) // 2, 2)

    def device(x_, y_, z_, h_):
        return {"img": lax.rem(y_, 2) * 2 + h_, "cls": (x_ * Z + z_) * 2 + y_ // 2}

    def slice_of(x_, y_):
        return lax.rem((x_ + 1) // 2, 2) * 2 + lax.rem((y_ + 1) // 2, 2)

    other_core = device(x, y, z, 1 - h)
    along_x = [device(wrap(x + d, X), y, z, h) for d in range(1, 4)]
    along_y = [device(x, wrap(y + d, 4), z, h) for d in range(1, 4)]
    along_z = [device(x, y, wrap(z + d, Z), h) for d in range(1, Z)]
    chips = [(x, y), (xm, y), (x, ym), (xm, ym)]
    same_core = [device(a, b, z, h) for a, b in chips]
    cross_core = [device(a, b, z, 1 - h) for a, b in chips]

    barrier = pltpu.get_barrier_semaphore()
    partners = [other_core] + along_x + along_y + along_z + [same_core[3]] + cross_core[1:]
    for partner in partners:
        pl.semaphore_signal(barrier, inc=1, device_id=partner, device_id_type=MESH)

    fetch = pltpu.make_async_copy(images_hbm, im, local_sem.at[0])
    fetch.start()

    count = [0]
    sent = []

    def new_id():
        count[0] += 1
        return count[0] - 1

    def send(src, dst, ident, to):
        copy = pltpu.make_async_remote_copy(src_ref=src, dst_ref=dst, send_sem=send_sem.at[ident],
                                            recv_sem=recv_sem.at[ident], device_id=to, device_id_type=MESH)
        copy.start()
        sent.append(copy)

    def arrived(dst, ident):
        pltpu.make_async_remote_copy(src_ref=dst, dst_ref=dst, send_sem=send_sem.at[ident],
                                     recv_sem=recv_sem.at[ident], device_id=other_core,
                                     device_id_type=MESH).wait_recv()

    row = lax.broadcasted_iota(jnp.int32, (256, 128), 0)
    lane = lax.broadcasted_iota(jnp.int32, (256, 128), 1)
    column = (row >> 4) & 3
    base = ((((row >> 2) & 3) ^ (3 * (column >> 1))) * 128 + (column >> 1) * 64 + (row >> 6) * 4 + (row & 3))
    for v in range(2):
        start = jnp.where(((column ^ (column >> 1)) & 1) == v, base, -4096)
        for s in range(2):
            for si in range(4):
                goes = start ^ (((si ^ (3 * s)) << 7) | (si << 4))
                for c in range(4):
                    regroup[v * 2 + s, si * 256:si * 256 + 256, c * 128:c * 128 + 128] = jnp.where(
                        goes == lane + c * 128, 1.0, 0.0).astype(BF16)
    for s in range(2):
        strip = refs_ref[:, pl.ds(pl.multiple_of((3 * s + yl * (1 - 2 * s)) * 1024, 1024), 1024)]
        placed = jnp.dot(strip, regroup[lax.rem(yl + h, 2) * 2 + s], preferred_element_type=F32)
        for c in range(4):
            ref_slab[c * 4:c * 4 + 4, s * 128:s * 128 + 128] = placed[:, c * 128:c * 128 + 128]
    zgot[z] = ref_slab[...].astype(BF16)
    meta[0, h, 0:1, :] = jnp.concatenate([noise_ref[...]] * 2, axis=1)
    meta[0, h, 1:5, :] = jnp.concatenate([assign_ref[...].astype(F32)] * 2, axis=1)
    meta[0, h, 5:9, :] = jnp.concatenate([turn_ref[...].astype(F32)] * 2, axis=1)

    pl.semaphore_wait(barrier, len(partners))

    ident_z = [new_id() for _ in range(Z - 1)]
    for d in range(1, Z):
        send(zgot.at[z], zgot.at[z], ident_z[d - 1], along_z[d - 1])

    fetch.wait()
    for hh in range(2):
        for u in range(2):
            for s in range(2):
                at = STRIP[u][s] * 1024
                placed = jnp.dot(im[:, at:at + 1024], regroup[(u ^ hh) * 2 + s], preferred_element_type=F32)
                for c in range(4):
                    blocks[hh, c, u, :, s * 128:s * 128 + 128] = placed[:, c * 128:c * 128 + 128].astype(BF16)
    mine = pl.ds(pl.multiple_of(h * 64, 64), 64)
    theirs = pl.ds(pl.multiple_of((1 - h) * 64, 64), 64)
    ident_im, ident_meta = new_id(), new_id()
    send(blocks.at[1 - h], xall.at[:, :, mine, :], ident_im, other_core)
    send(meta.at[0, h], meta.at[0, h], ident_meta, other_core)
    quad_im = [[new_id() for _ in range(2)] for _ in range(3)]
    quad_meta = [[new_id() for _ in range(2)] for _ in range(3)]
    for e in range(1, 4):
        c = slice_of(*chips[e])
        into = pl.ds(pl.multiple_of(e * 128 + h * 64, 64), 64)
        for k, (hh, to) in enumerate(((h, same_core[e]), (1 - h, cross_core[e]))):
            send(blocks.at[hh, c], xquad.at[:, into, :], quad_im[e - 1][k], to)
            send(meta.at[0, h], meta.at[e, h], quad_meta[e - 1][k], to)
    for c in range(4):
        for u in range(2):
            xall[c, u, mine, :] = blocks[h, c, u]

    for d in range(1, Z):
        arrived(zgot.at[wrap(z - d, Z)], ident_z[d - 1])

    def rows(x_, y_):
        return pl.ds(pl.multiple_of((y_ // 2) * 128 + x_ * 32, 32), 32)

    def region(part_, x_, y_):
        return refs.at[pl.ds(lax.rem(y_, 2) * 4 + part_ * 2, 2), rows(x_, y_), :]

    for q in range(Z):
        piece = zgot[q].astype(F32)
        for b in range(4):
            zline[b, q * 4:q * 4 + 4, :] = piece[b * 4:b * 4 + 4, :]
    for b in range(4):
        refs[yl * 4 + b, rows(x, y), :] = zline[b].astype(BF16)

    first_a, first_b = [new_id() for _ in range(3)], [new_id() for _ in range(3)]
    second_a = [[new_id() for _ in range(3)] for _ in range(4)]
    second_b = [[new_id() for _ in range(3)] for _ in range(4)]
    for d in range(3):
        send(region(0, x, y), region(0, x, y), first_a[d], along_x[d])
        send(region(1, x, y), region(1, x, y), first_b[d], along_y[d])
    for e in range(4):
        xe, ye = wrap(x - e, X), wrap(y - e, 4)
        if e:
            arrived(region(0, xe, y), first_a[e - 1])
        for d in range(3):
            send(region(0, xe, y), region(0, xe, y), second_a[e][d], along_y[d])
        if e:
            arrived(region(1, x, ye), first_b[e - 1])
        for d in range(3):
            send(region(1, x, ye), region(1, x, ye), second_b[e][d], along_x[d])

    swapped = ((row >> 6) & 1) * 128 + ((row >> 7) & 1) * 64 + (row & 3) * 4 + ((row >> 2) & 3)
    swapped = swapped + ((((row >> 4) & 3) ^ (3 * ((row >> 6) & 1)) ^ (3 * ((row >> 7) & 1))) << 4)
    for r, (swap, flips) in enumerate(FORMS):
        for c in range(4):
            goes = (swapped ^ (flips ^ (c << 4))) if swap else (row ^ flips)
            for half in range(2):
                inner[r, c, :, half * 128:half * 128 + 128] = jnp.where(goes == lane + half * 128, 1.0, 0.0).astype(BF16)
    arrived(xall.at[:, :, theirs, :], ident_im)
    for r, (swap, flips) in enumerate(FORMS):
        for u in range(2):
            source = u + swap * h * (1 - 2 * u)
            for c in range(4):
                turned[u * 4 + c, r * 128:r * 128 + 128, :] = jnp.dot(
                    xall[c, source], inner[r, c], preferred_element_type=F32).astype(BF16)
    for e in range(1, 4):
        for k, hh in enumerate((h, 1 - h)):
            into = pl.ds(pl.multiple_of(e * 128 + hh * 64, 64), 64)
            arrived(xquad.at[:, into, :], quad_im[e - 1][k])
            arrived(meta.at[e, hh], quad_meta[e - 1][k])
    for u in range(2):
        xquad[u, 0:128, :] = xall[own_c, u]
    for r, (swap, flips) in enumerate(FORMS):
        for u in range(2):
            source = u + swap * h * (1 - 2 * u)
            full = jnp.dot(xquad[source], inner[r, own_c], preferred_element_type=F32).astype(BF16)
            for e in range(4):
                turned_quad[u, e * 1024 + r * 128:e * 1024 + r * 128 + 128, :] = full[e * 128:e * 128 + 128]

    arrived(meta.at[0, 1 - h], ident_meta)
    kappa = lax.broadcasted_iota(jnp.int32, (K, 128), 0)
    label = (((kappa >> 2) & 31) * 8 + (kappa >> 7) * 4 + (kappa & 3)).astype(F32)
    info = [jnp.where(lane[0:16] < 64, meta[e, 0], meta[e, 1]) for e in range(4)]
    for e in range(4):
        tied = jnp.full((K, 128), -1.0, F32)
        for j in range(4):
            tied = jnp.where(label == info[e][1 + j:2 + j, :], info[e][5 + j:6 + j, :], tied)
        tie[e] = tied
    per_noise = 1.0 / info[0][0:1, :]

    for e in range(4):
        for d in range(3):
            arrived(region(0, wrap(x - e, X), wrap(y - d - 1, 4)), second_a[e][d])
            arrived(region(1, wrap(x - d - 1, X), wrap(y - e, 4)), second_b[e][d])

    square = jnp.zeros((K, 128), F32)
    for b in range(8):
        part_ref = refs[b].astype(F32)
        sq = part_ref * part_ref
        square = square + sq[:, :128] + sq[:, 128:]
    half_norm = 0.5 * jnp.sum(square, axis=1, keepdims=True)
    ident_s = [new_id() for _ in range(4)]
    for g in range(4):
        acc = jnp.zeros((K, 256), F32)
        for b in range(8):
            acc = acc + lax.dot_general(refs[b], turned[b, g * 256:g * 256 + 256, :], (((1,), (1,)), ((), ())),
                                        preferred_element_type=F32)
        own_scores[g] = acc - half_norm
        send(own_scores.at[g], other_scores.at[g], ident_s[g], other_core)
    for g in range(4):
        arrived(other_scores.at[g], ident_s[g])

    @pl.loop(0, 8)
    def _(i):
        chunk = pl.ds(pl.multiple_of(i * 32, 32), 32)
        score = []
        for g in range(4):
            both = own_scores[g, chunk, :] + other_scores[g, chunk, :]
            score += [both[:, :128] * per_noise, both[:, 128:] * per_noise]
        top = score[0]
        for s in score[1:]:
            top = jnp.maximum(top, s)
        total = jnp.exp(score[0] - top)
        for s in score[1:]:
            total = total + jnp.exp(s - top)
        per_class[chunk, :] = top + jnp.log(total)

    value = per_class[...]
    named = tie[0] >= 0.0
    best = jnp.max(jnp.where(named, value, -jnp.inf), axis=0, keepdims=True)
    expo = jnp.where(named, jnp.exp(jnp.where(named, value, best) - best), 0.0)
    weight = (expo / jnp.sum(expo, axis=0, keepdims=True)).astype(BF16).astype(F32)
    for j in range(4):
        wts[0, j:j + 1, :] = jnp.sum(jnp.where(label == info[0][1 + j:2 + j, :], weight, 0.0), axis=0, keepdims=True)
    ident_w = [new_id() for _ in range(3)]
    for e in range(1, 4):
        send(wts.at[0], wts.at[e], ident_w[e - 1], same_core[e])

    def fill(e, weight):
        for r in range(8):
            table[:, e * 1024 + r * 128:e * 1024 + r * 128 + 128] = jnp.where(tie[e] == r, weight, 0.0).astype(BF16)
        return lax.dot_general(jnp.ones((8, 128), BF16), weight.astype(BF16), (((1,), (1,)), ((), ())),
                               preferred_element_type=F32)

    totals = fill(0, weight)
    for u in range(2):
        part[u] = jnp.dot(table[:, 0:1024], turned_quad[u, 0:1024, :], preferred_element_type=F32)
    peak = jnp.max(value, axis=0, keepdims=True)
    evidence = peak + jnp.log(jnp.sum(jnp.exp(value - peak), axis=0, keepdims=True))
    evidence_ref[...] = jnp.where(h == 0, evidence[:, :64], evidence[:, 64:])
    for e in range(1, 4):
        arrived(wts.at[e], ident_w[e - 1])
        weight = jnp.zeros((K, 128), F32)
        for j in range(4):
            weight = jnp.where(label == info[e][1 + j:2 + j, :], wts[e, j:j + 1, :], weight)
        totals = totals + fill(e, weight)
    tot[...] = totals

    def part_rows(yh_, xp_):
        return pl.ds(pl.multiple_of(yh_ * 128 + xp_ * 64, 64), 64)

    across_x, across_y = device(xr, y, z, h), device(x, yr, z, h)
    ident_ty, ident_tx = new_id(), new_id()
    one_a, one_b, two_a, two_b = [new_id(), new_id()], [new_id(), new_id()], new_id(), new_id()
    send(tot, tot_y, ident_ty, across_y)
    part[0] = part[0] + jnp.dot(table[:, 1024:], turned_quad[0, 1024:, :], preferred_element_type=F32)
    send(part.at[0, part_rows(1 - yh, 1 - xp)], got_a.at[0], one_a[0], across_y)
    send(part.at[0, part_rows(1 - yh, xp)], got_a.at[1], one_a[1], across_y)
    part[1] = part[1] + jnp.dot(table[:, 1024:], turned_quad[1, 1024:, :], preferred_element_type=F32)
    send(part.at[1, part_rows(1 - yh, 1 - xp)], got_b.at[0], one_b[0], across_x)
    send(part.at[1, part_rows(yh, 1 - xp)], got_b.at[1], one_b[1], across_x)

    arrived(tot_y, ident_ty)
    lines[...] = tot[...] + tot_y[...]
    send(lines, tot_x, ident_tx, across_x)
    arrived(got_a.at[0], one_a[0])
    onward = part.at[0, part_rows(yh, 1 - xp)]
    onward[...] = onward[...] + got_a[0]
    send(onward, got_a2, two_a, across_x)
    arrived(got_b.at[0], one_b[0])
    onward = part.at[1, part_rows(1 - yh, xp)]
    onward[...] = onward[...] + got_b[0]
    send(onward, got_b2, two_b, across_y)
    arrived(got_a.at[1], one_a[1])
    whole_a = part[0, part_rows(yh, xp), :] + got_a[1]
    arrived(got_b.at[1], one_b[1])
    whole_b = part[1, part_rows(yh, xp), :] + got_b[1]
    arrived(tot_x, ident_tx)
    line = lines[...] + tot_x[...]
    arrived(got_a2, two_a)
    arrived(got_b2, two_b)

    for u, whole in enumerate((whole_a + got_a2[...], whole_b + got_b2[...])):
        for b in range(2):
            for q in range(Z):
                zsend[q, u * 8 + b * 4:u * 8 + b * 4 + 4, :] = whole[b * 32 + q * 4:b * 32 + q * 4 + 4, :]
    for q in range(Z):
        zsend[q, 16:24, :] = line
    ident_zr = [new_id() for _ in range(Z - 1)]
    for d in range(1, Z):
        send(zsend.at[wrap(z + d, Z)], zrecv.at[d - 1], ident_zr[d - 1], along_z[d - 1])
    final = zsend[z]
    for d in range(Z - 1):
        arrived(zrecv.at[d], ident_zr[d])
        final = final + zrecv[d]

    for b in range(2):
        for u in range(2):
            leave[b, u * 4:u * 4 + 4, :] = final[u * 8 + b * 4:u * 8 + b * 4 + 4, :]
    own_slot = own_c * 2 + h
    ident_o = [[new_id() for _ in range(2)] for _ in range(4)]
    send(leave.at[xb], slots.at[own_slot], ident_o[0][1], cross_core[0])
    for e in range(1, 4):
        b = xb + (1 - 2 * xb) * (e % 2)
        send(leave.at[b], slots.at[own_slot], ident_o[e][0], same_core[e])
        send(leave.at[b], slots.at[own_slot], ident_o[e][1], cross_core[e])
    slots[own_slot] = leave[xb]
    place = lax.broadcasted_iota(jnp.int32, (8, 256), 1)
    own_class = yh * 128 + x * 32 + z * 4 + (lax.broadcasted_iota(jnp.int32, (8, 256), 0) & 3)
    total = jnp.sum(jnp.where(place == own_class, jnp.broadcast_to(final[16:17, :], (8, 256)), 0.0), axis=1,
                    keepdims=True)[0:4]
    for e in range(4):
        c = slice_of(*chips[e])
        if e:
            arrived(slots.at[c * 2 + h], ident_o[e][0])
        arrived(slots.at[c * 2 + 1 - h], ident_o[e][1])
    strips = [jnp.zeros((4, 1024), F32) for _ in range(4)]
    for v in range(2):
        for s in range(2):
            for hh in range(2):
                u = v ^ hh
                for c in range(4):
                    zline[c, hh * 4:hh * 4 + 4, 0:128] = slots[c * 2 + hh, u * 4:u * 4 + 4, s * 128:s * 128 + 128]
            left = jnp.concatenate([zline[c, 0:8, 0:128] for c in range(4)], axis=1)
            high = left.astype(BF16).astype(F32)
            middle = (left - high).astype(BF16).astype(F32)
            three = jnp.concatenate([high, middle, left - high - middle], axis=0).astype(BF16)
            placed = lax.dot_general(three, regroup[v * 2 + s], (((1,), (1,)), ((), ())), preferred_element_type=F32)
            placed = placed[0:8] + placed[8:16] + placed[16:24]
            for hh in range(2):
                bi = STRIP[v ^ hh][s]
                strips[bi] = strips[bi] + placed[hh * 4:hh * 4 + 4]
    for bi in range(4):
        at = bi * 1024
        out_ref[:, at:at + 1024] = (strips[bi] + prior_weight * refs_ref[:, at:at + 1024].astype(F32)) / (
            total + prior_weight)

    for copy in sent:
        copy.wait_send()
    assert count[0] <= send_sem.shape[0]


def per_device(images, noise_var, references, assign, rotations):
    count = images.shape[0]
    X, Z = 4, lax.axis_size("cls") // 8
    vmem = pl.BlockSpec(memory_space=pltpu.VMEM)
    out, evidence = pl.pallas_call(
        functools.partial(kernel, X, Z),
        out_shape=(jax.ShapeDtypeStruct((4, SIDE * SIDE), F32), jax.ShapeDtypeStruct((1, count), F32)),
        in_specs=[pl.BlockSpec(memory_space=pltpu.HBM), vmem, vmem, vmem, vmem],
        out_specs=(vmem, vmem),
        scratch_shapes=[
            pltpu.VMEM((count, SIDE * SIDE), BF16),
            pltpu.VMEM((8, 4, 256, 256), BF16),
            pltpu.VMEM((4, 1024, 512), BF16),
            pltpu.VMEM((2, 4, 2, count, 256), BF16),
            pltpu.VMEM((4, 2, 2 * count, 256), BF16),
            pltpu.VMEM((2, 8 * count, 256), BF16),
            pltpu.VMEM((8, 1024, 256), BF16),
            pltpu.VMEM((2, 4096, 256), BF16),
            pltpu.VMEM((4, 2, 16, 128), F32),
            pltpu.VMEM((16, 256), F32),
            pltpu.VMEM((Z, 16, 256), BF16),
            pltpu.VMEM((4, 32, 256), F32),
            pltpu.VMEM((8, K, 256), BF16),
            pltpu.VMEM((4, K, 256), F32),
            pltpu.VMEM((4, K, 256), F32),
            pltpu.VMEM((K, 128), F32),
            pltpu.VMEM((4, K, 128), F32),
            pltpu.VMEM((K, 4096), BF16),
            pltpu.VMEM((2, K, 256), F32),
            pltpu.VMEM((2, 64, 256), F32),
            pltpu.VMEM((2, 64, 256), F32),
            pltpu.VMEM((64, 256), F32),
            pltpu.VMEM((64, 256), F32),
            pltpu.VMEM((4, 8, 128), F32),
            pltpu.VMEM((8, 256), F32),
            pltpu.VMEM((8, 256), F32),
            pltpu.VMEM((8, 256), F32),
            pltpu.VMEM((8, 256), F32),
            pltpu.VMEM((Z, 24, 256), F32),
            pltpu.VMEM((Z - 1, 24, 256), F32),
            pltpu.VMEM((2, 8, 256), F32),
            pltpu.VMEM((8, 8, 256), F32),
            pltpu.SemaphoreType.DMA((1,)),
            pltpu.SemaphoreType.DMA((96,)),
            pltpu.SemaphoreType.DMA((96,)),
        ],
        compiler_params=pltpu.CompilerParams(collective_id=0, has_side_effects=True, vmem_limit_bytes=48 << 20),
        name="classify",
    )(images, references, noise_var[None, :], assign.T, rotations.T)
    return out, evidence[0]


def solution(mesh):
    in_specs = (
        P(("img", "cls"), None),
        P(("img", "cls")),
        P("cls", None),
        P(("img", "cls"), None),
        P(("img", "cls"), None),
    )
    out_specs = (P("cls", None), P(("img", "cls")))
    return jax.shard_map(
        per_device, mesh=mesh, in_specs=in_specs, out_specs=out_specs, check_vma=False
    )
```

profile of v0, /device:TPU:1, one launch (start us, length us, event | category | flops | bytes accessed | tf_op | source)
XLA Modules:
  0.0 60.4 jit_solution(14475633941305432577)
XLA Ops:
  0.6 0.0 copy-start.3
  0.6 0.0 copy-start.2
  0.7 0.0 copy-start.4
  0.7 0.7 %copy-done.3 = s32[64,4]{0,1:T(4,128)S(1)} copy-done((s32[64,4]{0,1:T(4,128)S(1)}, s32[64,4]{0,1:T(4,128)}, u32[]{:S(2)}) %copy-start.3) | copy-done | bytes 1048
  1.3 0.0 copy-done.2
  1.3 0.0 copy-done.4
  1.3 0.0 copy-start
  1.3 1.0 %copy-done = bf16[64,4096]{1,0:T(8,128)(2,1)S(1)} copy-done((bf16[64,4096]{1,0:T(8,128)(2,1)S(1)}, bf16[64,4096]{1,0:T(8,128)(2,1)}, u32[]{:S(2)}) %copy-start) | copy-done | bytes 524312
  2.4 0.0 copy-start.1
  2.4 0.8 %copy-done.1 = bf16[4,4096]{1,0:T(4,128)(2,1)S(1)} copy-done((bf16[4,4096]{1,0:T(4,128)(2,1)S(1)}, bf16[4,4096]{1,0:T(4,128)(2,1)}, u32[]{:S(2)}) %copy-start.1) | copy-done | bytes 32792
  3.1 56.1 %classify.1 = (f32[4,4096]{1,0:T(4,128)S(1)}, f32[1,64]{1,0:T(1,128)S(1)}) custom-call(bf16[64,4096]{1,0:T(8,128)(2,1)S(1)} %copy-done, bf16[4,4096]{1,0:T(4,128)(2,1)S(1)} %copy-done.1, f32[1,64]{1,0:T(1,128)S(1)} %bitcast.6, s32[4,64]{1,0:T(4,128)S(1)} %bitcast.4, s32[4,64]{1,0:T(4,128)S(1)} %bitcast.5), custom_call_target="tpu_custom_call" | custom-call | tf_op jit(solution)/shard_map/classify/pallas_call | solution.py:395
  59.3 0.6 %copy.9 = f32[4,4096]{1,0:T(4,128)} copy(f32[4,4096]{1,0:T(4,128)S(1)} %get-tuple-element.8) | data formatting | bytes 131072
  59.9 0.5 copy.10
Async XLA Ops:
  0.6 0.7 %copy-start.3 = (s32[64,4]{0,1:T(4,128)S(1)}, s32[64,4]{0,1:T(4,128)}, u32[]{:S(2)}) copy-start(s32[64,4]{0,1:T(4,128)} %param.9) | copy-start | bytes 3076
  0.6 0.7 %copy-start.2 = (s32[64,4]{0,1:T(4,128)S(1)}, s32[64,4]{0,1:T(4,128)}, u32[]{:S(2)}) copy-start(s32[64,4]{0,1:T(4,128)} %param.8) | copy-start | bytes 3076
  0.7 0.7 %copy-start.4 = (f32[64]{0:T(128)S(1)}, f32[64]{0:T(128)}, u32[]{:S(2)}) copy-start(f32[64]{0:T(128)} %param.6) | copy-start | bytes 772
  1.3 1.0 %copy-start = (bf16[64,4096]{1,0:T(8,128)(2,1)S(1)}, bf16[64,4096]{1,0:T(8,128)(2,1)}, u32[]{:S(2)}) copy-start(bf16[64,4096]{1,0:T(8,128)(2,1)} %images_hbm.1) | copy-start | bytes 1572868
  2.4 0.8 %copy-start.1 = (bf16[4,4096]{1,0:T(4,128)(2,1)S(1)}, bf16[4,4096]{1,0:T(4,128)(2,1)}, u32[]{:S(2)}) copy-start(bf16[4,4096]{1,0:T(4,128)(2,1)} %refs_ref.1) | copy-start | bytes 98308
where the time goes:
time: 60.6 us; the launch traced here: 60.4 us
  Pallas kernels  56.1 us (93%)
  local copies, waits for them, and re-layouts  3.62 us (6%)
  between operations  0.67 us (1%)
    pallas_call x1, Pallas kernels, per_device(): pl.pallas_call(functools.partial(kernel, X, Z), out_shape=(jax.ShapeDtype...  56.1 us
    unnamed x12, local copies, waits for them, and re-layouts  3.62 us

commit v1 on v0

--- a/solution.py
+++ b/solution.py
@@ -49,10 +49,10 @@
     return lax.rem(value + 2 * size, size)
 
 
-def kernel(X, Z, images_hbm, refs_ref, noise_ref, assign_ref, turn_ref, out_ref, evidence_ref,
-           im, inner, regroup, blocks, xall, xquad, turned, turned_quad, meta, ref_slab, zgot, zline, refs, own_scores,
-           other_scores, per_class, tie, table, part, got_a, got_b, got_a2, got_b2, wts, tot, tot_y, tot_x, lines, zsend,
-           zrecv, leave, slots, local_sem, send_sem, recv_sem):
+def kernel(X, Z, images_hbm, refs_hbm, noise_hbm, assign_hbm, turn_hbm, out_ref, evidence_ref,
+           im, refs_ref, noise_ref, assign_ref, turn_ref, inner, regroup, blocks, xall, xquad, turned, turned_quad, meta, ref_slab, zgot, zline, refs, own_scores,
+           other_scores, per_class, tie, table, part, got_a, got_b, got_a2, got_b2, wts, tot, tot_y, tot_x, lines, all_tot,
+           zsend, zrecv, leave, slots, local_sem, send_sem, recv_sem):
     img, cls = lax.axis_index("img"), lax.axis_index("cls")
     yl, h = img // 2, lax.rem(img, 2)
     yh, z, x = lax.rem(cls, 2), lax.rem(cls // 2, Z), cls // (2 * Z)
@@ -75,13 +75,17 @@
     same_core = [device(a, b, z, h) for a, b in chips]
     cross_core = [device(a, b, z, 1 - h) for a, b in chips]
 
+    far_first = sorted(range(1, Z), key=lambda d: -min(d, Z - d))
+
     barrier = pltpu.get_barrier_semaphore()
-    partners = [other_core] + along_x + along_y + along_z + [same_core[3]] + cross_core[1:]
-    for partner in partners:
+    partners = [other_core] + along_x + along_y + [same_core[3]] + cross_core[1:] + [along_z[d - 1] for d in far_first[::-1]]
+    for partner in reversed(partners):
         pl.semaphore_signal(barrier, inc=1, device_id=partner, device_id_type=MESH)
 
-    fetch = pltpu.make_async_copy(images_hbm, im, local_sem.at[0])
-    fetch.start()
+    fetch = [pltpu.make_async_copy(source, into, local_sem.at[k]) for k, (source, into) in enumerate((
+        (refs_hbm, refs_ref), (noise_hbm, noise_ref), (assign_hbm, assign_ref), (turn_hbm, turn_ref), (images_hbm, im)))]
+    for copy in fetch:
+        copy.start()
 
     count = [0]
     sent = []
@@ -113,6 +117,8 @@
                 for c in range(4):
                     regroup[v * 2 + s, si * 256:si * 256 + 256, c * 128:c * 128 + 128] = jnp.where(
                         goes == lane + c * 128, 1.0, 0.0).astype(BF16)
+    for copy in fetch[:4]:
+        copy.wait()
     for s in range(2):
         strip = refs_ref[:, pl.ds(pl.multiple_of((3 * s + yl * (1 - 2 * s)) * 1024, 1024), 1024)]
         placed = jnp.dot(strip, regroup[lax.rem(yl + h, 2) * 2 + s], preferred_element_type=F32)
@@ -126,10 +132,10 @@
     pl.semaphore_wait(barrier, len(partners))
 
     ident_z = [new_id() for _ in range(Z - 1)]
-    for d in range(1, Z):
+    for d in far_first:
         send(zgot.at[z], zgot.at[z], ident_z[d - 1], along_z[d - 1])
 
-    fetch.wait()
+    fetch[4].wait()
     for hh in range(2):
         for u in range(2):
             for s in range(2):
@@ -142,14 +148,6 @@
     ident_im, ident_meta = new_id(), new_id()
     send(blocks.at[1 - h], xall.at[:, :, mine, :], ident_im, other_core)
     send(meta.at[0, h], meta.at[0, h], ident_meta, other_core)
-    quad_im = [[new_id() for _ in range(2)] for _ in range(3)]
-    quad_meta = [[new_id() for _ in range(2)] for _ in range(3)]
-    for e in range(1, 4):
-        c = slice_of(*chips[e])
-        into = pl.ds(pl.multiple_of(e * 128 + h * 64, 64), 64)
-        for k, (hh, to) in enumerate(((h, same_core[e]), (1 - h, cross_core[e]))):
-            send(blocks.at[hh, c], xquad.at[:, into, :], quad_im[e - 1][k], to)
-            send(meta.at[0, h], meta.at[e, h], quad_meta[e - 1][k], to)
     for c in range(4):
         for u in range(2):
             xall[c, u, mine, :] = blocks[h, c, u]
@@ -173,18 +171,18 @@
     first_a, first_b = [new_id() for _ in range(3)], [new_id() for _ in range(3)]
     second_a = [[new_id() for _ in range(3)] for _ in range(4)]
     second_b = [[new_id() for _ in range(3)] for _ in range(4)]
-    for d in range(3):
+    for d in (1, 0, 2):
         send(region(0, x, y), region(0, x, y), first_a[d], along_x[d])
         send(region(1, x, y), region(1, x, y), first_b[d], along_y[d])
     for e in range(4):
         xe, ye = wrap(x - e, X), wrap(y - e, 4)
         if e:
             arrived(region(0, xe, y), first_a[e - 1])
-        for d in range(3):
+        for d in (1, 0, 2):
             send(region(0, xe, y), region(0, xe, y), second_a[e][d], along_y[d])
         if e:
             arrived(region(1, x, ye), first_b[e - 1])
-        for d in range(3):
+        for d in (1, 0, 2):
             send(region(1, x, ye), region(1, x, ye), second_b[e][d], along_x[d])
 
     swapped = ((row >> 6) & 1) * 128 + ((row >> 7) & 1) * 64 + (row & 3) * 4 + ((row >> 2) & 3)
@@ -201,35 +199,34 @@
             for c in range(4):
                 turned[u * 4 + c, r * 128:r * 128 + 128, :] = jnp.dot(
                     xall[c, source], inner[r, c], preferred_element_type=F32).astype(BF16)
-    for e in range(1, 4):
-        for k, hh in enumerate((h, 1 - h)):
-            into = pl.ds(pl.multiple_of(e * 128 + hh * 64, 64), 64)
-            arrived(xquad.at[:, into, :], quad_im[e - 1][k])
-            arrived(meta.at[e, hh], quad_meta[e - 1][k])
-    for u in range(2):
-        xquad[u, 0:128, :] = xall[own_c, u]
-    for r, (swap, flips) in enumerate(FORMS):
-        for u in range(2):
-            source = u + swap * h * (1 - 2 * u)
-            full = jnp.dot(xquad[source], inner[r, own_c], preferred_element_type=F32).astype(BF16)
-            for e in range(4):
-                turned_quad[u, e * 1024 + r * 128:e * 1024 + r * 128 + 128, :] = full[e * 128:e * 128 + 128]
-
     arrived(meta.at[0, 1 - h], ident_meta)
     kappa = lax.broadcasted_iota(jnp.int32, (K, 128), 0)
     label = (((kappa >> 2) & 31) * 8 + (kappa >> 7) * 4 + (kappa & 3)).astype(F32)
-    info = [jnp.where(lane[0:16] < 64, meta[e, 0], meta[e, 1]) for e in range(4)]
-    for e in range(4):
+
+    def tie_up(e):
+        info = jnp.where(lane[0:16] < 64, meta[e, 0], meta[e, 1])
         tied = jnp.full((K, 128), -1.0, F32)
         for j in range(4):
-            tied = jnp.where(label == info[e][1 + j:2 + j, :], info[e][5 + j:6 + j, :], tied)
+            tied = jnp.where(label == info[1 + j:2 + j, :], info[5 + j:6 + j, :], tied)
         tie[e] = tied
+        return info
+
+    info = [tie_up(0)]
     per_noise = 1.0 / info[0][0:1, :]
 
     for e in range(4):
         for d in range(3):
             arrived(region(0, wrap(x - e, X), wrap(y - d - 1, 4)), second_a[e][d])
             arrived(region(1, wrap(x - d - 1, X), wrap(y - e, 4)), second_b[e][d])
+
+    quad_im = [[new_id() for _ in range(2)] for _ in range(3)]
+    quad_meta = [[new_id() for _ in range(2)] for _ in range(3)]
+    for e in range(1, 4):
+        c = slice_of(*chips[e])
+        into = pl.ds(pl.multiple_of(e * 128 + h * 64, 64), 64)
+        for k, (hh, to) in enumerate(((h, same_core[e]), (1 - h, cross_core[e]))):
+            send(blocks.at[hh, c], xquad.at[:, into, :], quad_im[e - 1][k], to)
+            send(meta.at[0, h], meta.at[e, h], quad_meta[e - 1][k], to)
 
     square = jnp.zeros((K, 128), F32)
     for b in range(8):
@@ -278,11 +275,37 @@
         for r in range(8):
             table[:, e * 1024 + r * 128:e * 1024 + r * 128 + 128] = jnp.where(tie[e] == r, weight, 0.0).astype(BF16)
         return lax.dot_general(jnp.ones((8, 128), BF16), weight.astype(BF16), (((1,), (1,)), ((), ())),
-                               preferred_element_type=F32)
-
+                               preferred_element_type=F32)[0:1]
+
+    def add(e, u, where):
+        more = jnp.dot(table[where, e * 1024:e * 1024 + 1024], turned_quad[u, e * 1024:e * 1024 + 1024, :],
+                       preferred_element_type=F32)
+        part[u, where] = part[u, where] + more if e else more
+
+    def turn_quad(first, last):
+        for r, (swap, flips) in enumerate(FORMS):
+            for u in range(2):
+                source = u + swap * h * (1 - 2 * u)
+                full = jnp.dot(xquad[source, first * 128:last * 128], inner[r, own_c],
+                               preferred_element_type=F32).astype(BF16)
+                for e in range(first, last):
+                    turned_quad[u, e * 1024 + r * 128:e * 1024 + r * 128 + 128, :] = (
+                        full[(e - first) * 128:(e - first) * 128 + 128])
+
+    for u in range(2):
+        xquad[u, 0:128, :] = xall[own_c, u]
+    everything = slice(0, K)
     totals = fill(0, weight)
+    turn_quad(0, 1)
     for u in range(2):
-        part[u] = jnp.dot(table[:, 0:1024], turned_quad[u, 0:1024, :], preferred_element_type=F32)
+        add(0, u, everything)
+    for e in range(1, 4):
+        for k, hh in enumerate((h, 1 - h)):
+            into = pl.ds(pl.multiple_of(e * 128 + hh * 64, 64), 64)
+            arrived(xquad.at[:, into, :], quad_im[e - 1][k])
+            arrived(meta.at[e, hh], quad_meta[e - 1][k])
+    turn_quad(1, 4)
+    info += [tie_up(e) for e in range(1, 4)]
     peak = jnp.max(value, axis=0, keepdims=True)
     evidence = peak + jnp.log(jnp.sum(jnp.exp(value - peak), axis=0, keepdims=True))
     evidence_ref[...] = jnp.where(h == 0, evidence[:, :64], evidence[:, 64:])
@@ -292,6 +315,9 @@
         for j in range(4):
             weight = jnp.where(label == info[e][1 + j:2 + j, :], wts[e, j:j + 1, :], weight)
         totals = totals + fill(e, weight)
+        if e < 3:
+            for u in range(2):
+                add(e, u, everything)
     tot[...] = totals
 
     def part_rows(yh_, xp_):
@@ -301,12 +327,16 @@
     ident_ty, ident_tx = new_id(), new_id()
     one_a, one_b, two_a, two_b = [new_id(), new_id()], [new_id(), new_id()], new_id(), new_id()
     send(tot, tot_y, ident_ty, across_y)
-    part[0] = part[0] + jnp.dot(table[:, 1024:], turned_quad[0, 1024:, :], preferred_element_type=F32)
+    add(3, 0, pl.ds(pl.multiple_of((1 - yh) * 128, 128), 128))
     send(part.at[0, part_rows(1 - yh, 1 - xp)], got_a.at[0], one_a[0], across_y)
     send(part.at[0, part_rows(1 - yh, xp)], got_a.at[1], one_a[1], across_y)
-    part[1] = part[1] + jnp.dot(table[:, 1024:], turned_quad[1, 1024:, :], preferred_element_type=F32)
+    add(3, 1, part_rows(1 - yh, 1 - xp))
     send(part.at[1, part_rows(1 - yh, 1 - xp)], got_b.at[0], one_b[0], across_x)
+    add(3, 1, part_rows(yh, 1 - xp))
     send(part.at[1, part_rows(yh, 1 - xp)], got_b.at[1], one_b[1], across_x)
+    add(3, 0, pl.ds(pl.multiple_of(yh * 128, 128), 128))
+    add(3, 1, part_rows(1 - yh, xp))
+    add(3, 1, part_rows(yh, xp))
 
     arrived(tot_y, ident_ty)
     lines[...] = tot[...] + tot_y[...]
@@ -324,7 +354,10 @@
     arrived(got_b.at[1], one_b[1])
     whole_b = part[1, part_rows(yh, xp), :] + got_b[1]
     arrived(tot_x, ident_tx)
-    line = lines[...] + tot_x[...]
+    all_tot[z] = lines[...] + tot_x[...]
+    ident_zt = [new_id() for _ in range(Z - 1)]
+    for d in far_first:
+        send(all_tot.at[z], all_tot.at[z], ident_zt[d - 1], along_z[d - 1])
     arrived(got_a2, two_a)
     arrived(got_b2, two_b)
 
@@ -332,10 +365,8 @@
         for b in range(2):
             for q in range(Z):
                 zsend[q, u * 8 + b * 4:u * 8 + b * 4 + 4, :] = whole[b * 32 + q * 4:b * 32 + q * 4 + 4, :]
-    for q in range(Z):
-        zsend[q, 16:24, :] = line
     ident_zr = [new_id() for _ in range(Z - 1)]
-    for d in range(1, Z):
+    for d in far_first:
         send(zsend.at[wrap(z + d, Z)], zrecv.at[d - 1], ident_zr[d - 1], along_z[d - 1])
     final = zsend[z]
     for d in range(Z - 1):
@@ -347,16 +378,20 @@
             leave[b, u * 4:u * 4 + 4, :] = final[u * 8 + b * 4:u * 8 + b * 4 + 4, :]
     own_slot = own_c * 2 + h
     ident_o = [[new_id() for _ in range(2)] for _ in range(4)]
+    for e in (3, 2, 1):
+        b = xb + (1 - 2 * xb) * (e % 2)
+        send(leave.at[b], slots.at[own_slot], ident_o[e][1], cross_core[e])
+        send(leave.at[b], slots.at[own_slot], ident_o[e][0], same_core[e])
     send(leave.at[xb], slots.at[own_slot], ident_o[0][1], cross_core[0])
-    for e in range(1, 4):
-        b = xb + (1 - 2 * xb) * (e % 2)
-        send(leave.at[b], slots.at[own_slot], ident_o[e][0], same_core[e])
-        send(leave.at[b], slots.at[own_slot], ident_o[e][1], cross_core[e])
     slots[own_slot] = leave[xb]
     place = lax.broadcasted_iota(jnp.int32, (8, 256), 1)
     own_class = yh * 128 + x * 32 + z * 4 + (lax.broadcasted_iota(jnp.int32, (8, 256), 0) & 3)
-    total = jnp.sum(jnp.where(place == own_class, jnp.broadcast_to(final[16:17, :], (8, 256)), 0.0), axis=1,
-                    keepdims=True)[0:4]
+    for d in range(1, Z):
+        arrived(all_tot.at[wrap(z - d, Z)], ident_zt[d - 1])
+    line = all_tot[0]
+    for q in range(1, Z):
+        line = line + all_tot[q]
+    total = jnp.sum(jnp.where(place == own_class, jnp.broadcast_to(line, (8, 256)), 0.0), axis=1, keepdims=True)[0:4]
     for e in range(4):
         c = slice_of(*chips[e])
         if e:
@@ -395,10 +430,14 @@
     out, evidence = pl.pallas_call(
         functools.partial(kernel, X, Z),
         out_shape=(jax.ShapeDtypeStruct((4, SIDE * SIDE), F32), jax.ShapeDtypeStruct((1, count), F32)),
-        in_specs=[pl.BlockSpec(memory_space=pltpu.HBM), vmem, vmem, vmem, vmem],
+        in_specs=[pl.BlockSpec(memory_space=pl.ANY)] * 5,
         out_specs=(vmem, vmem),
         scratch_shapes=[
             pltpu.VMEM((count, SIDE * SIDE), BF16),
+            pltpu.VMEM((4, SIDE * SIDE), BF16),
+            pltpu.VMEM((1, count), F32),
+            pltpu.VMEM((4, count), jnp.int32),
+            pltpu.VMEM((4, count), jnp.int32),
             pltpu.VMEM((8, 4, 256, 256), BF16),
             pltpu.VMEM((4, 1024, 512), BF16),
             pltpu.VMEM((2, 4, 2, count, 256), BF16),
@@ -422,19 +461,20 @@
             pltpu.VMEM((64, 256), F32),
             pltpu.VMEM((64, 256), F32),
             pltpu.VMEM((4, 8, 128), F32),
-            pltpu.VMEM((8, 256), F32),
-            pltpu.VMEM((8, 256), F32),
-            pltpu.VMEM((8, 256), F32),
-            pltpu.VMEM((8, 256), F32),
-            pltpu.VMEM((Z, 24, 256), F32),
-            pltpu.VMEM((Z - 1, 24, 256), F32),
+            pltpu.VMEM((1, 256), F32),
+            pltpu.VMEM((1, 256), F32),
+            pltpu.VMEM((1, 256), F32),
+            pltpu.VMEM((1, 256), F32),
+            pltpu.VMEM((Z, 1, 256), F32),
+            pltpu.VMEM((Z, 16, 256), F32),
+            pltpu.VMEM((Z - 1, 16, 256), F32),
             pltpu.VMEM((2, 8, 256), F32),
             pltpu.VMEM((8, 8, 256), F32),
-            pltpu.SemaphoreType.DMA((1,)),
+            pltpu.SemaphoreType.DMA((5,)),
             pltpu.SemaphoreType.DMA((96,)),
             pltpu.SemaphoreType.DMA((96,)),
         ],
-        compiler_params=pltpu.CompilerParams(collective_id=0, has_side_effects=True, vmem_limit_bytes=48 << 20),
+        compiler_params=pltpu.CompilerParams(collective_id=0, has_side_effects=True, vmem_limit_bytes=60 << 20),
         name="classify",
     )(images, references, noise_var[None, :], assign.T, rotations.T)
     return out, evidence[0]

time: 60.6 us -> 56.8 us (0.937)
  Pallas kernels: 56.1 us -> 54 us
  local copies, waits for them, and re-layouts: 3.62 us -> 1.99 us
    pallas_call x1, Pallas kernels: 56.1 us -> 54 us  [per_device(): pl.pallas_call(functools.partial(kernel, X, Z), out_shape=(jax.ShapeDtype...]
    unnamed x12 -> x4, local copies, waits for them, and re-layouts: 3.62 us -> 1.99 us
where the time goes in v1:
time: 56.8 us; the launch traced here: 56.6 us
  Pallas kernels  54 us (95%)
  local copies, waits for them, and re-layouts  1.99 us (4%)
  between operations  0.65 us (1%)
    pallas_call x1, Pallas kernels, per_device(): pl.pallas_call(functools.partial(kernel, X, Z), out_shape=(jax.ShapeDtype...  54 us
    unnamed x4, local copies, waits for them, and re-layouts  1.99 us

profile of v1, /device:TPU:1, one launch (start us, length us, event | category | flops | bytes accessed | tf_op | source)
XLA Modules:
  0.0 56.6 jit_solution(16195099721848249793)
XLA Ops:
  0.6 54.0 %classify.1 = (f32[4,4096]{1,0:T(4,128)}, f32[1,64]{1,0:T(1,128)}) custom-call(bf16[64,4096]{1,0:T(8,128)(2,1)} %images_hbm.1, bf16[4,4096]{1,0:T(4,128)(2,1)} %refs_hbm.1, f32[1,64]{1,0:T(1,128)} %bitcast.6, s32[4,64]{1,0:T(4,128)} %bitcast.4, s32[4,64]{1,0:T(4,128)} %bitcast.5), custom_call_target="tpu_custom_call" | custom-call | tf_op jit(solution)/shard_map/classify/pallas_call | solution.py:430
  54.6 0.0 copy-start
  54.7 1.5 %copy.9 = f32[4,4096]{1,0:T(4,128)} copy(f32[4,4096]{1,0:T(4,128)} %get-tuple-element.8) | data formatting | bytes 131072
  56.1 0.0 copy-done
  56.1 0.5 copy.10
Async XLA Ops:
  54.6 1.5 %copy-start = (f32[1,64]{1,0:T(1,128)S(1)}, f32[1,64]{1,0:T(1,128)}, u32[]{:S(2)}) copy-start(f32[1,64]{1,0:T(1,128)} %get-tuple-element.5) | copy-start | bytes 772

commit v2 on v1

--- a/solution.py
+++ b/solution.py
@@ -221,7 +221,7 @@
 
     quad_im = [[new_id() for _ in range(2)] for _ in range(3)]
     quad_meta = [[new_id() for _ in range(2)] for _ in range(3)]
-    for e in range(1, 4):
+    for e in (3, 2, 1):
         c = slice_of(*chips[e])
         into = pl.ds(pl.multiple_of(e * 128 + h * 64, 64), 64)
         for k, (hh, to) in enumerate(((h, same_core[e]), (1 - h, cross_core[e]))):

time: 56.8 us -> 56.9 us (level)
  no operation moved by 1% of the time
where the time goes in v2:
time: 56.9 us; the launch traced here: 56.7 us
  Pallas kernels  54.1 us (95%)
  local copies, waits for them, and re-layouts  1.99 us (3%)
  between operations  0.65 us (1%)
    pallas_call x1, Pallas kernels, per_device(): pl.pallas_call(functools.partial(kernel, X, Z), out_shape=(jax.ShapeDtype...  54.1 us
    unnamed x4, local copies, waits for them, and re-layouts  1.99 us

profile of v2, /device:TPU:1, one launch (start us, length us, event | category | flops | bytes accessed | tf_op | source)
XLA Modules:
  0.0 56.7 jit_solution(15520187185950554638)
XLA Ops:
  0.6 54.1 %classify.1 = (f32[4,4096]{1,0:T(4,128)}, f32[1,64]{1,0:T(1,128)}) custom-call(bf16[64,4096]{1,0:T(8,128)(2,1)} %images_hbm.1, bf16[4,4096]{1,0:T(4,128)(2,1)} %refs_hbm.1, f32[1,64]{1,0:T(1,128)} %bitcast.6, s32[4,64]{1,0:T(4,128)} %bitcast.4, s32[4,64]{1,0:T(4,128)} %bitcast.5), custom_call_target="tpu_custom_call" | custom-call | tf_op jit(solution)/shard_map/classify/pallas_call | solution.py:430
  54.8 0.0 copy-start
  54.8 1.5 %copy.9 = f32[4,4096]{1,0:T(4,128)} copy(f32[4,4096]{1,0:T(4,128)} %get-tuple-element.8) | data formatting | bytes 131072
  56.2 0.0 copy-done
  56.2 0.5 copy.10
Async XLA Ops:
  54.8 1.5 %copy-start = (f32[1,64]{1,0:T(1,128)S(1)}, f32[1,64]{1,0:T(1,128)}, u32[]{:S(2)}) copy-start(f32[1,64]{1,0:T(1,128)} %get-tuple-element.5) | copy-start | bytes 772
